TPU v7x, 32 devices: a whole 2x2x4 slice. The times are simulated.
32 devices in a mesh: seq: 16 (over z, x, core), chan: 2 (over y).
Axes of the slice: x: 2, y: 2, z: 4, core: 2. Of those that a mesh axis runs over, the one named last changes fastest.
Arguments:
- inputs: bfloat16 [131072, 2048], P('seq', 'chan'), may hold values from -6 to 6
- twiddle: float32 [256, 512], P('seq'), may hold values from -4 to 4
- right_factor: bfloat16 [512, 512], replicated, may hold values from -0.25 to 0.25
- left_factor: bfloat16 [256, 256], replicated, may hold values from -0.375 to 0.375
- blocks: bfloat16 [2048, 512], P('chan'), may hold values from -0.25 to 0.25
- block_mixer: float32 [512, 4, 4], replicated, may hold values from -3 to 3
- out_grad: bfloat16 [131072, 2048], P('seq', 'chan'), may hold values from -6 to 6
Outputs:
- output: bfloat16 [131072, 2048], P('seq', 'chan')
- input_grad: bfloat16 [131072, 2048], P('seq', 'chan')
All inputs are finite; a program needn't handle non-finite values.
Results may differ from a plain program's by a relative error of at most 0.0076.
Values may be sent and summed in bfloat16 or wider, within the bound.
A program may use at most 256 MiB of HBM per device.

v0:
```python
import jax
import jax.numpy as jnp
from jax import lax
from jax.sharding import PartitionSpec as P


def seq_pass(values, left_matrix):
    mixed_cols = jnp.einsum(
        "ia,ajc->ijc",
        left_matrix,
        lax.all_to_all(values, "seq", split_axis=1, concat_axis=0, tiled=True),
        preferred_element_type=jnp.float32,
    ).astype(jnp.bfloat16)
    return lax.all_to_all(mixed_cols, "seq", split_axis=0, concat_axis=1, tiled=True)


def send_back(values):
    return (
        lax.all_to_all(values[0], "chan", split_axis=2, concat_axis=1, tiled=True),
        lax.all_to_all(values[1], "chan", split_axis=2, concat_axis=1, tiled=True),
    )


def gate_of(values, rows_all, block_mixer):
    row_count, length, full_width = values.shape
    block_width = rows_all.shape[1]
    block_count = full_width // block_width
    block_table = rows_all.reshape(block_count, block_width, block_width)
    split = values.reshape(row_count, length, block_count, block_width)
    middle = jnp.einsum(
        "nbpq,pkq->nbpk", split, block_table, preferred_element_type=jnp.float32
    ).astype(jnp.bfloat16)
    gate = jnp.einsum(
        "nbpk,kop->nbok", middle.astype(jnp.float32), block_mixer, precision=lax.Precision.HIGHEST
    )
    return gate.reshape(row_count, length, full_width).astype(jnp.bfloat16)


def grad_of(values, rows_all, block_mixer):
    row_count, length, full_width = values.shape
    block_width = rows_all.shape[1]
    block_count = full_width // block_width
    block_table = rows_all.reshape(block_count, block_width, block_width)
    split = values.reshape(row_count, length, block_count, block_width).astype(jnp.float32)
    grad_middle = jnp.einsum(
        "nbok,kop->nbpk", split, block_mixer, precision=lax.Precision.HIGHEST
    ).astype(jnp.bfloat16)
    chan_grad = jnp.einsum(
        "nbpk,pkq->nbpq", grad_middle, block_table, preferred_element_type=jnp.float32
    )
    return chan_grad.reshape(row_count, length, full_width).astype(jnp.bfloat16)


def local(inputs, twiddle, right_factor, left_factor, blocks, block_mixer, out_grad):
    outer_rows, inner_len = twiddle.shape
    local_chan = inputs.shape[1]
    values = inputs.reshape(outer_rows, inner_len, local_chan)
    grad_values = out_grad.reshape(outer_rows, inner_len, local_chan)
    rows_all = lax.all_gather(blocks, "chan", axis=0, tiled=True)
    first_section = jnp.einsum(
        "jb,abc->ajc", right_factor, values, preferred_element_type=jnp.float32
    )
    twisted = (first_section * twiddle[:, :, None]).astype(jnp.bfloat16)
    mixed = seq_pass(twisted, left_factor)
    mixed_wide = mixed.astype(jnp.float32)
    grad_wide = grad_values.astype(jnp.float32)
    grad_gate = (grad_wide * mixed_wide).astype(jnp.bfloat16)
    gate, chan_grad = send_back(
        (
            gate_of(
                lax.all_to_all(values, "chan", split_axis=1, concat_axis=2, tiled=True),
                rows_all,
                block_mixer,
            ),
            grad_of(
                lax.all_to_all(grad_gate, "chan", split_axis=1, concat_axis=2, tiled=True),
                rows_all,
                block_mixer,
            ),
        )
    )
    gate_wide = gate.astype(jnp.float32)
    output = (gate_wide * mixed_wide).astype(jnp.bfloat16)
    grad_mixed = (grad_wide * gate_wide).astype(jnp.bfloat16)
    grad_twisted = seq_pass(grad_mixed, left_factor.T)
    grad_first = (grad_twisted.astype(jnp.float32) * twiddle[:, :, None]).astype(jnp.bfloat16)
    seq_grad = jnp.einsum(
        "jb,ajc->abc", right_factor, grad_first, preferred_element_type=jnp.float32
    )
    input_grad = (seq_grad + chan_grad.astype(jnp.float32)).astype(jnp.bfloat16)
    total_rows = outer_rows * inner_len
    return (output.reshape(total_rows, local_chan), input_grad.reshape(total_rows, local_chan))


def solution(mesh):
    return jax.shard_map(
        local,
        mesh=mesh,
        in_specs=(
            P("seq", "chan"),
            P("seq", None),
            P(),
            P(),
            P("chan", None),
            P(),
            P("seq", "chan"),
        ),
        out_specs=(P("seq", "chan"), P("seq", "chan")),
        check_vma=False,
    )
```

profile of v0, /device:TPU:11, one launch (start us, length us, event | category | flops | bytes accessed | tf_op | source)
XLA Modules:
  0.0 2424.3 jit_solution(1132671157621040498)
XLA Ops:
  7.2 18.7 copy.88
  25.9 9.9 all-to-all-start
  35.8 18.4 fusion.5
  54.2 23.7 copy.99
  78.0 139.4 %all-to-all-done = bf16[16,512,1024]{2,0,1:T(8,128)(2,1)} async-done(((bf16[16,512,1024]{2,0,1:T(8,128)(2,1)}), bf16[16,512,1024]{2,0,1:T(8,128)(2,1)}, u32[]{:S(2)}, u32[]{:S(2)}) %all-to-all-start) | async-done | bytes 16777248 | tf_op jit(solution)/shard_map/all_to_all | solution.py:71
  217.4 7.4 all-to-all-start.2
  226.0 23.8 copy.90
  249.9 10.2 all-gather.2.cloned.1.call-done
  260.0 16.0 convert_bitcast_fusion.9
  276.1 57.1 %convert_bitcast_fusion.8 = bf16[16,256,4,512]{1,2,0,3:T(4,128)(2,1)S(1)} fusion(f32[512,4,4,1]{1,2,3,0:T(4,128)S(1)} %copy.129, bf16[16,256,4,512]{1,3,0,2:T(8,128)(2,1)} %convert_bitcast_fusion.9), kind=kOutput, calls=%fused_computation.32 | convolution fusion | flops 411041792 | bytes 33587200 | tf_op jit(solution)/shard_map/nbpk,kop->nbok/dot_general | solution.py:33
  333.2 9.7 copy.134
  342.9 244.0 %all-to-all-done.2 = bf16[16,512,1024]{2,0,1:T(8,128)(2,1)} async-done(((bf16[16,512,1024]{2,0,1:T(8,128)(2,1)}), bf16[16,512,1024]{2,0,1:T(8,128)(2,1)}, u32[]{:S(2)}, u32[]{:S(2)}) %all-to-all-start.2) | async-done | bytes 16777248 | tf_op jit(solution)/shard_map/all_to_all | solution.py:11
  587.0 9.7 all-to-all-start.1
  596.7 18.7 copy.101
  615.4 42.4 %convert_bitcast_fusion.7 = bf16[256,32,1024]{0,2,1:T(8,128)(2,1)} fusion(bf16[256,32,1024]{2,1,0:T(8,128)(2,1)} %bitcast.98, bf16[256,256]{1,0:T(8,128)(2,1)S(1)} %copy-done.3), kind=kOutput, calls=%fused_computation.31 | convolution fusion | flops 4303355904 | bytes 33685504 | tf_op jit(solution)/shard_map/ia,ajc->ijc/dot_general | solution.py:8
  657.8 23.4 copy.103
  681.2 97.7 %all-to-all-done.1 = bf16[16,256,2048]{1,0,2:T(8,128)(2,1)} async-done(((bf16[16,256,2048]{1,0,2:T(8,128)(2,1)}), bf16[16,256,2048]{1,0,2:T(8,128)(2,1)}, u32[]{:S(2)}, u32[]{:S(2)}) %all-to-all-start.1) | async-done | bytes 16777248 | tf_op jit(solution)/shard_map/all_to_all | solution.py:19
  784.6 10.3 copy.96
  794.8 11.5 convert_bitcast_fusion.3
  806.4 31.9 %copy.97 = f32[16,2,256,1024]{3,2,1,0:T(8,128)} copy(f32[16,2,256,1024]{2,3,1,0:T(8,128)} %convert_bitcast_fusion.3) | data formatting | bytes 67108864 | tf_op jit(solution)/shard_map/convert_element_type | solution.py:82
  838.3 308.4 %all-to-all-done.3 = bf16[256,32,1024]{2,1,0:T(8,128)(2,1)} async-done(((bf16[256,32,1024]{2,1,0:T(8,128)(2,1)}), bf16[256,32,1024]{2,1,0:T(8,128)(2,1)}, u32[]{:S(2)}, u32[]{:S(2)}) %all-to-all-start.3) | async-done | bytes 16777248 | tf_op jit(solution)/shard_map/all_to_all | solution.py:14
  1146.7 9.4 convert_bitcast_fusion.2
  1156.1 11.1 copy.104
  1167.1 33.0 %fusion = (bf16[16,512,1024]{2,1,0:T(8,128)(2,1)}, bf16[16,512,1024]{2,1,0:T(8,128)(2,1)S(1)}) fusion(bf16[16,512,1024]{2,1,0:T(8,128)(2,1)} %bitcast.103, f32[16,2,256,1024]{3,2,1,0:T(8,128)} %copy.97, f32[16,16,32,1024]{3,2,1,0:T(8,128)} %copy.104), kind=kLoop, calls=%fused_computation.2 | loop fusion | flops 41943040 | bytes 117440512 | tf_op jit(solution)/shard_map/convert_element_type | solution.py:84
  1200.1 26.9 %copy.114 = bf16[16,512,1024]{2,0,1:T(8,128)(2,1)} copy(bf16[16,512,1024]{2,1,0:T(8,128)(2,1)S(1)} %get-tuple-element.3) | data formatting | bytes 33554432 | tf_op jit(solution)/shard_map/convert_element_type | solution.py:67
  1227.0 9.8 all-to-all-start.6
  1236.8 18.7 copy.106
  1255.5 163.4 %all-to-all-done.6 = bf16[16,512,1024]{2,0,1:T(8,128)(2,1)} async-done(((bf16[16,512,1024]{2,0,1:T(8,128)(2,1)}), bf16[16,512,1024]{2,0,1:T(8,128)(2,1)}, u32[]{:S(2)}, u32[]{:S(2)}) %all-to-all-start.6) | async-done | bytes 16777248 | tf_op jit(solution)/shard_map/all_to_all | solution.py:76
  1419.0 6.1 all-to-all-start.4
  1425.0 23.2 copy.116
  1448.3 46.0 %convert_bitcast_fusion.5 = bf16[16,256,4,512]{1,2,0,3:T(4,128)(2,1)} fusion(f32[512,4,4,1]{1,2,3,0:T(4,128)S(1)} %copy-done.2, bf16[16,256,4,512]{1,3,2,0:T(8,128)(2,1)} %bitcast.107), kind=kOutput, calls=%fused_computation.29 | convolution fusion | flops 411041792 | bytes 33587200 | tf_op jit(solution)/shard_map/nbok,kop->nbpk/dot_general | solution.py:45
  1494.2 25.7 %convert_bitcast_fusion.4 = bf16[16,256,4,512]{3,1,0,2:T(8,128)(2,1)} fusion(bf16[4,512,512,1]{2,1,3,0:T(8,128)(2,1)S(1)} %bitcast.112, bf16[16,256,4,512]{1,2,0,3:T(4,128)(2,1)} %convert_bitcast_fusion.5), kind=kOutput, calls=%fused_computation.28 | convolution fusion | flops 8598323200 | bytes 35651584 | tf_op jit(solution)/shard_map/nbpk,pkq->nbpq/dot_general | solution.py:48
  1520.0 27.9 %copy.141 = bf16[16,256,4,512]{1,0,3,2:T(8,128)(2,1)} copy(bf16[16,256,4,512]{3,1,0,2:T(8,128)(2,1)} %convert_bitcast_fusion.4) | data formatting | bytes 33554432 | tf_op jit(solution)/shard_map/convert_element_type | solution.py:51
  1547.8 239.2 %all-to-all-done.4 = bf16[16,512,1024]{2,0,1:T(8,128)(2,1)} async-done(((bf16[16,512,1024]{2,0,1:T(8,128)(2,1)}), bf16[16,512,1024]{2,0,1:T(8,128)(2,1)}, u32[]{:S(2)}, u32[]{:S(2)}) %all-to-all-start.4) | async-done | bytes 16777248 | tf_op jit(solution)/shard_map/all_to_all | solution.py:11
  1787.0 9.7 all-to-all-start.7
  1796.7 18.7 copy.108
  1815.4 31.5 %convert_bitcast_fusion.6 = bf16[256,32,1024]{0,2,1:T(8,128)(2,1)} fusion(bf16[256,32,1024]{2,1,0:T(8,128)(2,1)} %bitcast.108, bf16[256,256]{1,0:T(8,128)(2,1)S(1)} %copy-done.4), kind=kOutput, calls=%fused_computation.30 | convolution fusion | flops 4303355904 | bytes 33685504 | tf_op jit(solution)/shard_map/ia,ajc->ijc/dot_general | solution.py:8
  1846.9 23.4 copy.110
  1870.3 108.6 %all-to-all-done.7 = bf16[16,256,2048]{1,0,2:T(8,128)(2,1)} async-done(((bf16[16,256,2048]{1,0,2:T(8,128)(2,1)}), bf16[16,256,2048]{1,0,2:T(8,128)(2,1)}, u32[]{:S(2)}, u32[]{:S(2)}) %all-to-all-start.7) | async-done | bytes 16777248 | tf_op jit(solution)/shard_map/all_to_all | solution.py:20
  1984.6 27.6 %fusion.4 = bf16[8192,1024]{1,0:T(8,128)(2,1)} fusion(f32[16,16,32,1024]{3,2,1,0:T(8,128)} %copy.104, f32[16,2,256,1024]{3,2,1,0:T(8,128)} %copy.97), kind=kLoop, calls=%fused_computation.13 | loop fusion | flops 16777216 | bytes 83886080 | tf_op jit(solution)/shard_map/convert_element_type | solution.py:83
  2012.2 10.2 copy.122
  2022.4 11.5 convert_bitcast_fusion
  2034.0 31.9 %copy.123 = f32[16,2,256,1024]{3,2,1,0:T(8,128)} copy(f32[16,2,256,1024]{2,3,1,0:T(8,128)} %convert_bitcast_fusion) | data formatting | bytes 67108864 | tf_op jit(solution)/shard_map/convert_element_type | solution.py:90
  2065.9 280.8 %all-to-all-done.5 = bf16[256,32,1024]{2,1,0:T(8,128)(2,1)} async-done(((bf16[256,32,1024]{2,1,0:T(8,128)(2,1)}), bf16[256,32,1024]{2,1,0:T(8,128)(2,1)}, u32[]{:S(2)}, u32[]{:S(2)}) %all-to-all-start.5) | async-done | bytes 16777248 | tf_op jit(solution)/shard_map/all_to_all | solution.py:14
  2346.7 9.4 convert_bitcast_fusion.1
  2356.1 11.1 copy.111
  2367.1 17.4 fusion.3
  2384.5 32.7 %fusion.2 = bf16[16,512,1024]{2,1,0:T(8,128)(2,1)} fusion(f32[16,2,256,1024]{3,2,1,0:T(8,128)} %copy.123, bf16[16,512,1024]{2,1,0:T(8,128)(2,1)} %fusion.3, bf16[512,512]{1,0:T(8,128)(2,1)S(1)} %copy-done), kind=kOutput, calls=%fused_computation.7 | convolution fusion | flops 8606711808 | bytes 67633152 | tf_op jit(solution)/shard_map/jb,ajc->abc/dot_general | solution.py:87
  (23 shorter events, 12.6 us)
Async XLA Ops:
  7.2 28.6 %copy-start = (bf16[512,512]{1,0:T(8,128)(2,1)S(1)}, bf16[512,512]{1,0:T(8,128)(2,1)}, u32[]{:S(2)}) copy-start(bf16[512,512]{1,0:T(8,128)(2,1)} %param.9) | copy-start | bytes 1572868
  25.9 9.9 copy-start.6
  25.9 191.5 %all-to-all-start = ((bf16[16,512,1024]{2,0,1:T(8,128)(2,1)}), bf16[16,512,1024]{2,0,1:T(8,128)(2,1)}, u32[]{:S(2)}, u32[]{:S(2)}) async-start(bf16[16,512,1024]{2,0,1:T(8,128)(2,1)} %copy.88), calls=%async_computation | async-start | bytes 33554432 | tf_op jit(solution)/shard_map/all_to_all | solution.py:71
  78.0 147.6 %copy-start.5 = (f32[512,4,4]{0,2,1:T(4,128)S(1)}, f32[512,4,4]{0,2,1:T(4,128)}, u32[]{:S(2)}) copy-start(f32[512,4,4]{0,2,1:T(4,128)} %param.12) | copy-start | bytes 98308
  217.4 369.5 %all-to-all-start.2 = ((bf16[16,512,1024]{2,0,1:T(8,128)(2,1)}), bf16[16,512,1024]{2,0,1:T(8,128)(2,1)}, u32[]{:S(2)}, u32[]{:S(2)}) async-start(bf16[16,512,1024]{2,0,1:T(8,128)(2,1)} %copy.99), calls=%async_computation.2 | async-start | bytes 33554432 | tf_op jit(solution)/shard_map/all_to_all | solution.py:11
  224.8 35.2 %all-gather.2.cloned.1.call-start = ((), (), s32[]{:S(2)}) async-start(), calls=%async_computation.8 | async-start | bytes 3145728 | tf_op jit(solution)/shard_map/all_gather | solution.py:59
  226.0 50.0 %copy-start.1 = (f32[512,4,4,1]{1,2,3,0:T(4,128)}, f32[512,4,4,1]{1,2,3,0:T(4,128)S(1)}, u32[]{:S(2)}) copy-start(f32[512,4,4,1]{1,2,3,0:T(4,128)S(1)} %copy.129) | copy-start | bytes 98308
  587.0 191.9 %all-to-all-start.1 = ((bf16[16,256,2048]{1,0,2:T(8,128)(2,1)}), bf16[16,256,2048]{1,0,2:T(8,128)(2,1)}, u32[]{:S(2)}, u32[]{:S(2)}) async-start(bf16[16,256,2048]{1,0,2:T(8,128)(2,1)} %bitcast.101), calls=%async_computation.1 | async-start | bytes 33554432 | tf_op jit(solution)/shard_map/all_to_all | solution.py:19
  596.7 18.7 copy-start.3
  778.9 367.8 %all-to-all-start.3 = ((bf16[256,32,1024]{2,1,0:T(8,128)(2,1)}), bf16[256,32,1024]{2,1,0:T(8,128)(2,1)}, u32[]{:S(2)}, u32[]{:S(2)}) async-start(bf16[256,32,1024]{2,1,0:T(8,128)(2,1)} %copy.103), calls=%async_computation.3 | async-start | bytes 33554432 | tf_op jit(solution)/shard_map/all_to_all | solution.py:14
  1227.0 191.9 %all-to-all-start.6 = ((bf16[16,512,1024]{2,0,1:T(8,128)(2,1)}), bf16[16,512,1024]{2,0,1:T(8,128)(2,1)}, u32[]{:S(2)}, u32[]{:S(2)}) async-start(bf16[16,512,1024]{2,0,1:T(8,128)(2,1)} %copy.114), calls=%async_computation.6 | async-start | bytes 33554432 | tf_op jit(solution)/shard_map/all_to_all | solution.py:76
  1419.0 368.0 %all-to-all-start.4 = ((bf16[16,512,1024]{2,0,1:T(8,128)(2,1)}), bf16[16,512,1024]{2,0,1:T(8,128)(2,1)}, u32[]{:S(2)}, u32[]{:S(2)}) async-start(bf16[16,512,1024]{2,0,1:T(8,128)(2,1)} %copy.106), calls=%async_computation.4 | async-start | bytes 33554432 | tf_op jit(solution)/shard_map/all_to_all | solution.py:11
  1425.0 23.2 copy-start.2
  1448.3 46.0 %copy-start.8 = (bf16[2048,512]{1,0:T(8,128)(2,1)S(1)}, bf16[2048,512]{1,0:T(8,128)(2,1)}, u32[]{:S(2)}) copy-start(bf16[2048,512]{1,0:T(8,128)(2,1)} %all-gather.2.cloned.1.call-done) | copy-start | bytes 6291460
  1787.0 191.9 %all-to-all-start.7 = ((bf16[16,256,2048]{1,0,2:T(8,128)(2,1)}), bf16[16,256,2048]{1,0,2:T(8,128)(2,1)}, u32[]{:S(2)}, u32[]{:S(2)}) async-start(bf16[16,256,2048]{1,0,2:T(8,128)(2,1)} %bitcast.102), calls=%async_computation.7 | async-start | bytes 33554432 | tf_op jit(solution)/shard_map/all_to_all | solution.py:20
  1796.7 18.7 copy-start.4
  1978.9 367.8 %all-to-all-start.5 = ((bf16[256,32,1024]{2,1,0:T(8,128)(2,1)}), bf16[256,32,1024]{2,1,0:T(8,128)(2,1)}, u32[]{:S(2)}, u32[]{:S(2)}) async-start(bf16[256,32,1024]{2,1,0:T(8,128)(2,1)} %copy.110), calls=%async_computation.5 | async-start | bytes 33554432 | tf_op jit(solution)/shard_map/all_to_all | solution.py:14
  2356.0 11.1 copy-start.7
Sparse Core Ops, SparseCore 0:
  227.2 32.7 all-gather.1
where the time goes:
time: 2440 us; the launch traced here: 2420 us
  waiting for transfers between devices  1590 us (65%)
  local copies, waits for them, and re-layouts  364 us (15%)
  matrix products  270 us (11%)
  other arithmetic  120 us (5%)
  starting transfers between devices  64.6 us (3%)
    all_to_all x2, waiting for transfers between devices, seq_pass(): lax.all_to_all(mixed_cols, 'seq', split_axis=0, concat_axis=1, tiled=True)  589 us
    all_to_all x2, waiting for transfers between devices, seq_pass(): lax.all_to_all(values, 'seq', split_axis=1, concat_axis=0, tiled=True)  483 us
    all_to_all x1, waiting for transfers between devices, local(): lax.all_to_all(grad_gate, 'chan', split_axis=1, concat_axis=2, tiled=True)  163 us
    all_to_all x1, waiting for transfers between devices, local(): lax.all_to_all(values, 'chan', split_axis=1, concat_axis=2, tiled=True)  139 us
    all_to_all x1, waiting for transfers between devices, send_back(): lax.all_to_all(values[1], 'chan', split_axis=2, concat_axis=1, tiled=True)  109 us
    all_to_all x1, waiting for transfers between devices, send_back(): lax.all_to_all(values[0], 'chan', split_axis=2, concat_axis=1, tiled=True)  97.7 us
    dot_general x2, matrix products, seq_pass(): jnp.einsum('ia,ajc->ijc', left_matrix, lax.all_to_all(values, 'seq', spli...  73.9 us
    dot_general x1, matrix products, gate_of(): jnp.einsum('nbpk,kop->nbok', middle.astype(jnp.float32), block_mixer, pre...  57.1 us
  transfers between devices with their start and end apart: 9, of which 9 were waited for; matrix products, arithmetic and copies ran while one was open for 24% of the time, Pallas kernels for 0%

commit v1 on v0

--- a/solution.py
+++ b/solution.py
@@ -3,14 +3,18 @@
 from jax import lax
 from jax.sharding import PartitionSpec as P
 
+F32, BF16 = jnp.float32, jnp.bfloat16
 
-def seq_pass(values, left_matrix):
+
+def seq_pass(values, left_matrix, after=None):
     mixed_cols = jnp.einsum(
         "ia,ajc->ijc",
         left_matrix,
         lax.all_to_all(values, "seq", split_axis=1, concat_axis=0, tiled=True),
-        preferred_element_type=jnp.float32,
-    ).astype(jnp.bfloat16)
+        preferred_element_type=F32,
+    ).astype(BF16)
+    if after is not None:
+        mixed_cols, _ = lax.optimization_barrier((mixed_cols, after))
     return lax.all_to_all(mixed_cols, "seq", split_axis=0, concat_axis=1, tiled=True)
 
 
@@ -51,7 +55,7 @@
     return chan_grad.reshape(row_count, length, full_width).astype(jnp.bfloat16)
 
 
-def local(inputs, twiddle, right_factor, left_factor, blocks, block_mixer, out_grad):
+def split_blocks(inputs, twiddle, right_factor, left_factor, blocks, block_mixer, out_grad):
     outer_rows, inner_len = twiddle.shape
     local_chan = inputs.shape[1]
     values = inputs.reshape(outer_rows, inner_len, local_chan)
@@ -92,6 +96,76 @@
     return (output.reshape(total_rows, local_chan), input_grad.reshape(total_rows, local_chan))
 
 
+def local(inputs, twiddle, right_factor, left_factor, blocks, block_mixer, out_grad):
+    outer_rows, inner_len = twiddle.shape
+    local_chan = inputs.shape[1]
+    width = blocks.shape[1]
+    if local_chan % width:
+        return split_blocks(
+            inputs, twiddle, right_factor, left_factor, blocks, block_mixer, out_grad
+        )
+    parts = local_chan // width
+    chan_size = lax.axis_size("chan")
+    me = lax.axis_index("chan")
+    values = inputs.reshape(outer_rows, inner_len, local_chan)
+    grad_values = out_grad.reshape(outer_rows, inner_len, local_chan)
+    x = [values[:, :, i * width:(i + 1) * width] for i in range(parts)]
+    grad = [grad_values[:, :, i * width:(i + 1) * width] for i in range(parts)]
+    table = [blocks[i * width:(i + 1) * width] for i in range(parts)]
+    number = [[(me + chan_size - r) % chan_size * parts + i for i in range(parts)] for r in range(chan_size)]
+
+    def from_all(arrays):
+        held = [arrays]
+        for r in range(1, chan_size):
+            perm = [(d, (d + r) % chan_size) for d in range(chan_size)]
+            held.append([lax.ppermute(a, "chan", perm) for a in arrays])
+        return held
+
+    def mix(held, coefs):
+        total = 0.0
+        for r in range(chan_size):
+            for i in range(parts):
+                row = lax.dynamic_index_in_dim(coefs, number[r][i], axis=0, keepdims=False)
+                total = total + held[r][i].astype(F32) * row[None, None, :]
+        return total.astype(BF16)
+
+    def mixer_row(axis, index):
+        return lax.dynamic_index_in_dim(jnp.transpose(block_mixer, (1, 2, 0)), index, axis=axis, keepdims=False)
+
+    middle = [
+        jnp.einsum("nbq,kq->nbk", x[i], table[i], preferred_element_type=F32).astype(BF16)
+        for i in range(parts)
+    ]
+    middle_all = from_all(middle)
+    mixed = []
+    for i in range(parts):
+        first_section = jnp.einsum("jb,abc->ajc", right_factor, x[i], preferred_element_type=F32)
+        twisted = (first_section * twiddle[:, :, None]).astype(BF16)
+        mixed.append(seq_pass(twisted, left_factor))
+    gate = [mix(middle_all, mixer_row(0, number[0][i])) for i in range(parts)]
+
+    grad_gate = [(grad[i].astype(F32) * mixed[i].astype(F32)).astype(BF16) for i in range(parts)]
+    grad_gate_all = from_all(grad_gate)
+    output, input_grad = [], []
+    seq_grad = []
+    for i in range(parts):
+        gate_wide = gate[i].astype(F32)
+        output.append((gate_wide * mixed[i].astype(F32)).astype(BF16))
+        grad_mixed = (grad[i].astype(F32) * gate_wide).astype(BF16)
+        grad_twisted = seq_pass(grad_mixed, left_factor.T, grad_gate[i])
+        grad_first = (grad_twisted.astype(F32) * twiddle[:, :, None]).astype(BF16)
+        seq_grad.append(jnp.einsum("jb,ajc->abc", right_factor, grad_first, preferred_element_type=F32))
+    for i in range(parts):
+        grad_middle = mix(grad_gate_all, mixer_row(1, number[0][i]))
+        chan_grad = jnp.einsum("nbk,kq->nbq", grad_middle, table[i], preferred_element_type=F32).astype(BF16)
+        input_grad.append((seq_grad[i] + chan_grad.astype(F32)).astype(BF16))
+    total_rows = outer_rows * inner_len
+    return (
+        jnp.concatenate(output, axis=2).reshape(total_rows, local_chan),
+        jnp.concatenate(input_grad, axis=2).reshape(total_rows, local_chan),
+    )
+
+
 def solution(mesh):
     return jax.shard_map(
         local,

time: 2440 us -> 2040 us (0.84)
  waiting for transfers between devices: 1590 us -> 1300 us
  matrix products: 270 us -> 185 us
  other arithmetic: 120 us -> 149 us
  local copies, waits for them, and re-layouts: 364 us -> 338 us
    all_to_all x4 -> x0, waiting for transfers between devices: 509 us -> none  [the longest x1 163 us: local(): lax.all_to_all(grad_gate, 'chan', split_axis=1, concat_axis=2, tiled=True)]
    ppermute x0 -> x4, waiting for transfers between devices: none -> 435 us  [from_all(): held.append([lax.ppermute(a, 'chan', perm) for a in arrays])]
    all_to_all x2 -> x4, waiting for transfers between devices: 589 us -> 411 us  [seq_pass(): lax.all_to_all(mixed_cols, 'seq', split_axis=0, concat_axis=1, tiled=True)]
    dot_general x5 -> x6, matrix products: 163 us -> 84.4 us  [the longest x2 43.1 us: local(): jnp.einsum('nbk,kq->nbq', grad_middle, table[i], preferred_element_type=F32)]
    all_to_all x4 -> x0, local copies, waits for them, and re-layouts: 67.6 us -> none  [the longest x1 23.8 us: local(): lax.all_to_all(values, 'chan', split_axis=1, concat_axis=2, tiled=True)]
    convert_element_type x9 -> x10, local copies, waits for them, and re-layouts: 193 us -> 146 us  [the longest x4 59.9 us: local(): output.append((gate_wide * mixed[i].astype(F32)).astype(BF16))]
    concatenate x0 -> x2, local copies, waits for them, and re-layouts: none -> 43.1 us  [the longest x1 21.5 us: local(): jnp.concatenate(output, axis=2).reshape(total_rows, local_chan)]
    all_to_all x4 -> x0, starting transfers between devices: 39.1 us -> none  [the longest x1 9.87 us: local(): lax.all_to_all(values, 'chan', split_axis=1, concat_axis=2, tiled=True)]
  transfers between devices with their start and end apart: 9 -> 12, of which waited for: 9 -> 10; matrix products, arithmetic and copies ran while one was open for 24% -> 28% of each run, Pallas kernels for 0% -> 0%
where the time goes in v1:
time: 2040 us; the launch traced here: 2020 us
  waiting for transfers between devices  1300 us (64%)
  local copies, waits for them, and re-layouts  338 us (17%)
  matrix products  185 us (9%)
  other arithmetic  149 us (7%)
  starting transfers between devices  47.9 us (2%)
    all_to_all x4, waiting for transfers between devices, seq_pass(): lax.all_to_all(values, 'seq', split_axis=1, concat_axis=0, tiled=True)  456 us
    ppermute x4, waiting for transfers between devices, from_all(): held.append([lax.ppermute(a, 'chan', perm) for a in arrays])  435 us
    all_to_all x4, waiting for transfers between devices, seq_pass(): lax.all_to_all(mixed_cols, 'seq', split_axis=0, concat_axis=1, tiled=True)  411 us
    dot_general x4, matrix products, seq_pass(): jnp.einsum('ia,ajc->ijc', left_matrix, lax.all_to_all(values, 'seq', spli...  80.5 us
    convert_element_type x4, local copies, waits for them, and re-layouts, local(): output.append((gate_wide * mixed[i].astype(F32)).astype(BF16))  59.9 us
    all_to_all x4, local copies, waits for them, and re-layouts, seq_pass(): lax.all_to_all(values, 'seq', split_axis=1, concat_axis=0, tiled=True)  49.9 us
    dot_general x2, matrix products, local(): jnp.einsum('nbk,kq->nbq', grad_middle, table[i], preferred_element_type=F32)  43.1 us
  transfers between devices with their start and end apart: 12, of which 10 were waited for; matrix products, arithmetic and copies ran while one was open for 28% of the time, Pallas kernels for 0%

profile of v1, /device:TPU:11, one launch (start us, length us, event | category | flops | bytes accessed | tf_op | source)
XLA Modules:
  0.0 2022.4 jit_solution(5556804982878275798)
XLA Ops:
  12.1 14.8 copy.68
  43.8 15.0 copy.60
  58.8 157.0 %all-to-all-done.2 = bf16[16,512,512]{2,0,1:T(8,128)(2,1)} async-done(((bf16[16,512,512]{2,0,1:T(8,128)(2,1)}), bf16[16,512,512]{2,0,1:T(8,128)(2,1)}, u32[]{:S(2)}, u32[]{:S(2)}) %all-to-all-start.2) | async-done | bytes 8388640 | tf_op jit(solution)/shard_map/all_to_all | solution.py:13
  254.8 12.3 copy.114
  267.1 12.3 copy.113
  280.0 133.7 %collective-permute-done.1 = bf16[16,512,512]{1,2,0:T(8,128)(2,1)} collective-permute-done((bf16[16,512,512]{1,2,0:T(8,128)(2,1)}, bf16[16,512,512]{1,2,0:T(8,128)(2,1)}, u32[]{:S(2)}, u32[]{:S(2)}) %collective-permute-start.1) | collective-permute-done | bytes 8388640 | tf_op jit(solution)/shard_map/ppermute | solution.py:121
  413.7 179.8 %collective-permute-done = bf16[16,512,512]{1,2,0:T(8,128)(2,1)} collective-permute-done((bf16[16,512,512]{1,2,0:T(8,128)(2,1)}, bf16[16,512,512]{1,2,0:T(8,128)(2,1)}, u32[]{:S(2)}, u32[]{:S(2)}) %collective-permute-start) | collective-permute-done | bytes 8388640 | tf_op jit(solution)/shard_map/ppermute | solution.py:121
  593.5 30.0 %fusion.10 = (bf16[16,512,512]{1,2,0:T(8,128)(2,1)}, bf16[16,512,512]{1,2,0:T(8,128)(2,1)}, bf16[16,512,512]{1,2,0:T(8,128)(2,1)}, bf16[16,512,512]{1,2,0:T(8,128)(2,1)}) fusion(bf16[16,512,512]{1,2,0:T(8,128)(2,1)} %copy.113, f32[512]{0:T(512)S(1)} %bitcast.129, bf16[16,512,512]{1,2,0:T(8,128)(2,1)} %collective-permute-done.1, f32[512]{0:T(512)S(1)} %bitcast.130, ...), kind=kLoop, calls=%fused_computation.32 | loop fusion | flops 117440512 | bytes 83902464 | tf_op jit(solution)/shard_map/convert_element_type | solution.py:154
  623.5 14.9 copy.77
  645.3 14.9 copy.89
  660.2 167.4 %all-to-all-done.4 = bf16[16,512,512]{2,0,1:T(8,128)(2,1)} async-done(((bf16[16,512,512]{2,0,1:T(8,128)(2,1)}), bf16[16,512,512]{2,0,1:T(8,128)(2,1)}, u32[]{:S(2)}, u32[]{:S(2)}) %all-to-all-start.4) | async-done | bytes 8388640 | tf_op jit(solution)/shard_map/all_to_all | solution.py:13
  832.7 12.5 copy.62
  845.2 23.5 %convert_bitcast_fusion.7 = bf16[256,32,512]{0,2,1:T(8,128)(2,1)} fusion(bf16[256,32,512]{2,1,0:T(8,128)(2,1)} %bitcast.112, bf16[256,256]{1,0:T(8,128)(2,1)S(1)} %copy-done.3), kind=kOutput, calls=%fused_computation.79 | convolution fusion | flops 2151677952 | bytes 16908288 | tf_op jit(solution)/shard_map/ia,ajc->ijc/dot_general | solution.py:10
  868.7 14.6 copy.64
  883.3 131.6 %all-to-all-done.6 = bf16[16,512,512]{2,0,1:T(8,128)(2,1)} async-done(((bf16[16,512,512]{2,0,1:T(8,128)(2,1)}), bf16[16,512,512]{2,0,1:T(8,128)(2,1)}, u32[]{:S(2)}, u32[]{:S(2)}) %all-to-all-start.6) | async-done | bytes 8388640 | tf_op jit(solution)/shard_map/all_to_all | solution.py:13
  1020.2 12.5 copy.70
  1032.7 23.5 %convert_bitcast_fusion.6 = bf16[256,32,512]{0,2,1:T(8,128)(2,1)} fusion(bf16[256,32,512]{2,1,0:T(8,128)(2,1)} %bitcast.113, bf16[256,256]{1,0:T(8,128)(2,1)S(1)} %copy-done.3), kind=kOutput, calls=%fused_computation.76 | convolution fusion | flops 2151677952 | bytes 16908288 | tf_op jit(solution)/shard_map/ia,ajc->ijc/dot_general | solution.py:10
  1056.1 14.7 copy.72
  1070.8 131.4 %all-to-all-done.1 = bf16[256,32,512]{2,1,0:T(8,128)(2,1)} async-done(((bf16[256,32,512]{2,1,0:T(8,128)(2,1)}), bf16[256,32,512]{2,1,0:T(8,128)(2,1)}, u32[]{:S(2)}, u32[]{:S(2)}) %all-to-all-start.1) | async-done | bytes 8388640 | tf_op jit(solution)/shard_map/all_to_all | solution.py:18
  1207.3 12.5 copy.79
  1219.8 16.9 convert_bitcast_fusion.5
  1236.7 12.0 convert_bitcast_fusion.3
  1248.7 12.4 copy.65
  1261.0 17.6 copy.66
  1278.6 17.1 fusion.11
  1295.8 14.6 copy.82
  1310.4 79.0 %all-to-all-done.3 = bf16[256,32,512]{2,1,0:T(8,128)(2,1)} async-done(((bf16[256,32,512]{2,1,0:T(8,128)(2,1)}), bf16[256,32,512]{2,1,0:T(8,128)(2,1)}, u32[]{:S(2)}, u32[]{:S(2)}) %all-to-all-start.3) | async-done | bytes 8388640 | tf_op jit(solution)/shard_map/all_to_all | solution.py:18
  1394.5 12.5 copy.91
  1407.0 16.7 convert_bitcast_fusion.4
  1423.6 12.0 convert_bitcast_fusion.2
  1435.6 12.4 copy.73
  1448.0 17.6 copy.74
  1465.6 17.1 fusion.20
  1482.7 14.7 copy.93
  1497.4 79.3 %all-to-all-done.5 = bf16[256,32,512]{2,1,0:T(8,128)(2,1)} async-done(((bf16[256,32,512]{2,1,0:T(8,128)(2,1)}), bf16[256,32,512]{2,1,0:T(8,128)(2,1)}, u32[]{:S(2)}, u32[]{:S(2)}) %all-to-all-start.5) | async-done | bytes 8388640 | tf_op jit(solution)/shard_map/all_to_all | solution.py:18
  1583.7 13.6 pad_maximum_fusion
  1597.3 21.5 %copy.75 = bf16[16,512,1024]{2,1,0:T(8,128)(2,1)} copy(bf16[16,512,1024]{1,2,0:T(8,128)(2,1)} %pad_maximum_fusion) | data formatting | bytes 33554432 | tf_op jit(solution)/shard_map/concatenate | solution.py:164
  1618.9 12.0 convert_bitcast_fusion.1
  1630.8 12.2 copy.83
  1643.1 121.6 %all-to-all-done.7 = bf16[256,32,512]{2,1,0:T(8,128)(2,1)} async-done(((bf16[256,32,512]{2,1,0:T(8,128)(2,1)}), bf16[256,32,512]{2,1,0:T(8,128)(2,1)}, u32[]{:S(2)}, u32[]{:S(2)}) %all-to-all-start.7) | async-done | bytes 8388640 | tf_op jit(solution)/shard_map/all_to_all | solution.py:18
  1764.6 12.0 convert_bitcast_fusion
  1776.6 14.1 copy.94
  1802.8 11.9 fusion.76
  1822.8 121.1 %collective-permute-done.3 = bf16[16,512,512]{1,2,0:T(8,128)(2,1)} collective-permute-done((bf16[16,512,512]{1,2,0:T(8,128)(2,1)}, bf16[16,512,512]{1,2,0:T(8,128)(2,1)}, u32[]{:S(2)}, u32[]{:S(2)}) %collective-permute-start.3) | collective-permute-done | bytes 8388640 | tf_op jit(solution)/shard_map/ppermute | solution.py:121
  1944.0 24.1 %fusion.22 = bf16[16,512,512]{1,2,0:T(8,128)(2,1)} fusion(f32[16,512,512]{2,1,0:T(8,128)} %fusion.76, bf16[16,512,512]{1,2,0:T(8,128)(2,1)} %get-tuple-element.12, bf16[16,512,512]{1,2,0:T(8,128)(2,1)} %get-tuple-element.14, bf16[16,512,512]{1,2,0:T(8,128)(2,1)} %collective-permute-done.2, bf16[16,512,512]{1,2,0:T(8,128)(2,1)} %collective-permute-done.3, ...), kind=kOutput, calls=%fused_computation.51 | convolution fusion | flops 4362076160 | bytes 59252736 | tf_op jit(solution)/shard_map/nbk,kq->nbq/dot_general | solution.py:160
  1968.2 19.0 fusion.24
  1987.2 13.6 pad_maximum_fusion.1
  2000.7 21.5 %copy.98 = bf16[16,512,1024]{2,1,0:T(8,128)(2,1)} copy(bf16[16,512,1024]{1,2,0:T(8,128)(2,1)} %pad_maximum_fusion.1) | data formatting | bytes 33554432 | tf_op jit(solution)/shard_map/concatenate | solution.py:165
  (62 shorter events, 122.7 us)
Async XLA Ops:
  0.6 1.0 copy-start
  12.1 21.4 %copy-start.4 = (f32[16,512]{1,0:T(8,128)S(1)}, f32[16,512]{1,0:T(8,128)}, u32[]{:S(2)}) copy-start(f32[16,512]{1,0:T(8,128)} %param.8) | copy-start | bytes 98308
  26.9 188.9 %all-to-all-start.2 = ((bf16[16,512,512]{2,0,1:T(8,128)(2,1)}), bf16[16,512,512]{2,0,1:T(8,128)(2,1)}, u32[]{:S(2)}, u32[]{:S(2)}) async-start(bf16[16,512,512]{2,0,1:T(8,128)(2,1)} %copy.68), calls=%async_computation.2 | async-start | bytes 16777216 | tf_op jit(solution)/shard_map/all_to_all | solution.py:13
  43.8 177.6 %copy-start.19 = (bf16[1024,512]{1,0:T(8,128)(2,1)S(1)}, bf16[1024,512]{1,0:T(8,128)(2,1)}, u32[]{:S(2)}) copy-start(bf16[1024,512]{1,0:T(8,128)(2,1)} %param.11) | copy-start | bytes 3145732
  215.8 422.7 %all-to-all-start = ((bf16[16,512,512]{2,0,1:T(8,128)(2,1)}), bf16[16,512,512]{2,0,1:T(8,128)(2,1)}, u32[]{:S(2)}, u32[]{:S(2)}) async-start(bf16[16,512,512]{2,0,1:T(8,128)(2,1)} %copy.60), calls=%async_computation | async-start | bytes 16777216 | tf_op jit(solution)/shard_map/all_to_all | solution.py:13
  231.7 182.0 %collective-permute-start.1 = (bf16[16,512,512]{1,2,0:T(8,128)(2,1)}, bf16[16,512,512]{1,2,0:T(8,128)(2,1)}, u32[]{:S(2)}, u32[]{:S(2)}) collective-permute-start(bf16[16,512,512]{1,2,0:T(8,128)(2,1)} %fusion.67), channel_id=1, source_target_pairs={{0,1},{1,0},{2,3},{3,2},{4,5},{5,4},{6,7},{7,6},{8,9},{9,8},{10,11... | collective-permute-start | bytes 25165832 | tf_op jit(solution)/shard_map/ppermute | solution.py:121
  243.2 350.3 %collective-permute-start = (bf16[16,512,512]{1,2,0:T(8,128)(2,1)}, bf16[16,512,512]{1,2,0:T(8,128)(2,1)}, u32[]{:S(2)}, u32[]{:S(2)}) collective-permute-start(bf16[16,512,512]{1,2,0:T(8,128)(2,1)} %fusion.64), channel_id=1, source_target_pairs={{0,1},{1,0},{2,3},{3,2},{4,5},{5,4},{6,7},{7,6},{8,9},{9,8},{10,11... | collective-permute-start | bytes 25165832 | tf_op jit(solution)/shard_map/ppermute | solution.py:121
  254.8 24.5 %copy-start.6 = (f32[512,4,4]{0,2,1:T(4,128)S(1)}, f32[512,4,4]{0,2,1:T(4,128)}, u32[]{:S(2)}) copy-start(f32[512,4,4]{0,2,1:T(4,128)} %param.12) | copy-start | bytes 98308
  280.0 343.5 %copy-start.7 = (f32[512,1,1]{0,2,1:T(1,128)}, f32[512,1,1]{0,2,1:T(1,128)S(1)}, u32[]{:S(2)}) copy-start(f32[512,1,1]{0,2,1:T(1,128)S(1)} %get-tuple-element.23) | copy-start | bytes 6148
  280.0 343.5 %copy-start.9 = (f32[512,1,1]{0,2,1:T(1,128)}, f32[512,1,1]{0,2,1:T(1,128)S(1)}, u32[]{:S(2)}) copy-start(f32[512,1,1]{0,2,1:T(1,128)S(1)} %get-tuple-element.27) | copy-start | bytes 6148
  280.0 343.5 %copy-start.11 = (f32[512,1,1]{0,2,1:T(1,128)}, f32[512,1,1]{0,2,1:T(1,128)S(1)}, u32[]{:S(2)}) copy-start(f32[512,1,1]{0,2,1:T(1,128)S(1)} %get-tuple-element.22) | copy-start | bytes 6148
  280.0 343.5 %copy-start.13 = (f32[512,1,1]{0,2,1:T(1,128)}, f32[512,1,1]{0,2,1:T(1,128)S(1)}, u32[]{:S(2)}) copy-start(f32[512,1,1]{0,2,1:T(1,128)S(1)} %get-tuple-element.26) | copy-start | bytes 6148
  638.5 189.2 %all-to-all-start.4 = ((bf16[16,512,512]{2,0,1:T(8,128)(2,1)}), bf16[16,512,512]{2,0,1:T(8,128)(2,1)}, u32[]{:S(2)}, u32[]{:S(2)}) async-start(bf16[16,512,512]{2,0,1:T(8,128)(2,1)} %copy.77), calls=%async_computation.4 | async-start | bytes 16777216 | tf_op jit(solution)/shard_map/all_to_all | solution.py:13
  660.2 185.0 %copy-start.3 = (bf16[256,256]{1,0:T(8,128)(2,1)S(1)}, bf16[256,256]{1,0:T(8,128)(2,1)}, u32[]{:S(2)}) copy-start(bf16[256,256]{1,0:T(8,128)(2,1)} %param.10) | copy-start | bytes 393220
  827.6 187.3 %all-to-all-start.6 = ((bf16[16,512,512]{2,0,1:T(8,128)(2,1)}), bf16[16,512,512]{2,0,1:T(8,128)(2,1)}, u32[]{:S(2)}, u32[]{:S(2)}) async-start(bf16[16,512,512]{2,0,1:T(8,128)(2,1)} %copy.89), calls=%async_computation.6 | async-start | bytes 16777216 | tf_op jit(solution)/shard_map/all_to_all | solution.py:13
  1014.9 187.3 %all-to-all-start.1 = ((bf16[256,32,512]{2,1,0:T(8,128)(2,1)}), bf16[256,32,512]{2,1,0:T(8,128)(2,1)}, u32[]{:S(2)}, u32[]{:S(2)}) async-start(bf16[256,32,512]{2,1,0:T(8,128)(2,1)} %copy.64), calls=%async_computation.1 | async-start | bytes 16777216 | tf_op jit(solution)/shard_map/all_to_all | solution.py:18
  1202.2 187.3 %all-to-all-start.3 = ((bf16[256,32,512]{2,1,0:T(8,128)(2,1)}), bf16[256,32,512]{2,1,0:T(8,128)(2,1)}, u32[]{:S(2)}, u32[]{:S(2)}) async-start(bf16[256,32,512]{2,1,0:T(8,128)(2,1)} %copy.72), calls=%async_computation.3 | async-start | bytes 16777216 | tf_op jit(solution)/shard_map/all_to_all | solution.py:18
  1389.4 187.3 %all-to-all-start.5 = ((bf16[256,32,512]{2,1,0:T(8,128)(2,1)}), bf16[256,32,512]{2,1,0:T(8,128)(2,1)}, u32[]{:S(2)}, u32[]{:S(2)}) async-start(bf16[256,32,512]{2,1,0:T(8,128)(2,1)} %copy.82), calls=%async_computation.5 | async-start | bytes 16777216 | tf_op jit(solution)/shard_map/all_to_all | solution.py:18
  1576.7 187.9 %all-to-all-start.7 = ((bf16[256,32,512]{2,1,0:T(8,128)(2,1)}), bf16[256,32,512]{2,1,0:T(8,128)(2,1)}, u32[]{:S(2)}, u32[]{:S(2)}) async-start(bf16[256,32,512]{2,1,0:T(8,128)(2,1)} %copy.93), calls=%async_computation.7 | async-start | bytes 16777216 | tf_op jit(solution)/shard_map/all_to_all | solution.py:18
  1582.2 240.7 %collective-permute-start.2 = (bf16[16,512,512]{1,2,0:T(8,128)(2,1)}, bf16[16,512,512]{1,2,0:T(8,128)(2,1)}, u32[]{:S(2)}, u32[]{:S(2)}) collective-permute-start(bf16[16,512,512]{1,2,0:T(8,128)(2,1)} %get-tuple-element.12), channel_id=1, source_target_pairs={{0,1},{1,0},{2,3},{3,2},{4,5},{5,4},{6,7},{7,6},{8,9},{9,8},{10,11... | collective-permute-start | bytes 25165832 | tf_op jit(solution)/shard_map/ppermute | solution.py:121
  1583.5 360.5 %collective-permute-start.3 = (bf16[16,512,512]{1,2,0:T(8,128)(2,1)}, bf16[16,512,512]{1,2,0:T(8,128)(2,1)}, u32[]{:S(2)}, u32[]{:S(2)}) collective-permute-start(bf16[16,512,512]{1,2,0:T(8,128)(2,1)} %get-tuple-element.14), channel_id=1, source_target_pairs={{0,1},{1,0},{2,3},{3,2},{4,5},{5,4},{6,7},{7,6},{8,9},{9,8},{10,11... | collective-permute-start | bytes 25165832 | tf_op jit(solution)/shard_map/ppermute | solution.py:121
  1776.6 16.4 copy-start.1
  1776.6 16.4 copy-start.5
  1814.7 129.3 %copy-start.12 = (f32[512,1,1]{0,2,1:T(1,128)S(1)}, f32[512,1,1]{0,2,1:T(1,128)}, u32[]{:S(2)}) copy-start(f32[512,1,1]{0,2,1:T(1,128)} %copy-done.11) | copy-start | bytes 6148
  1814.7 129.3 %copy-start.14 = (f32[512,1,1]{0,2,1:T(1,128)S(1)}, f32[512,1,1]{0,2,1:T(1,128)}, u32[]{:S(2)}) copy-start(f32[512,1,1]{0,2,1:T(1,128)} %copy-done.13) | copy-start | bytes 6148
  1814.7 129.3 %copy-start.17 = (f32[512,1,1]{0,2,1:T(1,128)S(1)}, f32[512,1,1]{0,2,1:T(1,128)}, u32[]{:S(2)}) copy-start(f32[512,1,1]{0,2,1:T(1,128)} %get-tuple-element.28) | copy-start | bytes 6148
  1814.7 129.3 %copy-start.18 = (f32[512,1,1]{0,2,1:T(1,128)S(1)}, f32[512,1,1]{0,2,1:T(1,128)}, u32[]{:S(2)}) copy-start(f32[512,1,1]{0,2,1:T(1,128)} %get-tuple-element.29) | copy-start | bytes 6148
  1944.0 24.1 %copy-start.2 = (f32[16,512,512]{2,1,0:T(8,128)S(1)}, f32[16,512,512]{2,1,0:T(8,128)}, u32[]{:S(2)}) copy-start(f32[16,512,512]{2,1,0:T(8,128)} %fusion.78) | copy-start | bytes 50331652
  1944.0 24.1 %copy-start.8 = (f32[512,1,1]{0,2,1:T(1,128)S(1)}, f32[512,1,1]{0,2,1:T(1,128)}, u32[]{:S(2)}) copy-start(f32[512,1,1]{0,2,1:T(1,128)} %copy-done.7) | copy-start | bytes 6148
  1944.0 24.1 %copy-start.10 = (f32[512,1,1]{0,2,1:T(1,128)S(1)}, f32[512,1,1]{0,2,1:T(1,128)}, u32[]{:S(2)}) copy-start(f32[512,1,1]{0,2,1:T(1,128)} %copy-done.9) | copy-start | bytes 6148
  1944.0 24.1 %copy-start.15 = (f32[512,1,1]{0,2,1:T(1,128)S(1)}, f32[512,1,1]{0,2,1:T(1,128)}, u32[]{:S(2)}) copy-start(f32[512,1,1]{0,2,1:T(1,128)} %get-tuple-element.18) | copy-start | bytes 6148
  1944.0 24.1 %copy-start.16 = (f32[512,1,1]{0,2,1:T(1,128)S(1)}, f32[512,1,1]{0,2,1:T(1,128)}, u32[]{:S(2)}) copy-start(f32[512,1,1]{0,2,1:T(1,128)} %get-tuple-element.19) | copy-start | bytes 6148
